TPU v7x, 256 devices: a whole 4x4x8 slice. The times are simulated.
256 devices in a mesh: blk: 16 (over x_lo, z), rep: 16 (over y, x_hi, core).
Axes of the slice: x: 4 (x_hi: 2, x_lo: 2; x = x_hi * 2 + x_lo), y: 4, z: 8, core: 2. Of those that a mesh axis runs over, the one named last changes fastest.
Arguments:
- a_blocks: bfloat16 [48, 16, 6, 128, 128], P('blk', None, None, None, 'rep'), may hold values from -0.5 to 0.5
- a_cols: int32 [48, 16, 6], P('blk'), may hold values from 0 to 111, as said below
- b_blocks: bfloat16 [1792, 16, 3, 128, 128], P('blk', 'rep'), may hold values from -6 to 6
- b_cols: int32 [1792, 16, 3], P('blk', 'rep'), may hold values from 0 to 111, as said below
- c_cols: int32 [48, 16, 4], P(None, 'rep'), may hold values from 0 to 111, as said below
Outputs:
- c_blocks: float32 [48, 16, 4, 128, 128], P('blk', 'rep')
Inputs may be any that keep to these rules, and one draw needn't show every extreme that they name: `a_cols`: within each block row and panel the 6 entries are distinct. `b_cols`: within each block row and tile the 3 entries are distinct. `c_cols`: within each block row and tile the 4 entries are distinct.
All inputs are finite; a program needn't handle non-finite values.
Results may differ from a plain program's by a relative error of at most 0.0003.
Values may be sent and summed in bfloat16 or wider, within the bound.
A program may use at most 128 MiB of HBM per device.

v0:
```python
import math
import jax
import jax.numpy as jnp
from jax import lax
from jax.sharding import PartitionSpec as P


def select_blocks(chosen, chosen_cols, wanted):
    hits = chosen_cols[..., :, None] == wanted
    total = None
    for slot_t in range(chosen.shape[-3]):
        term = jnp.where(
            hits[..., slot_t, :, None, None],
            chosen[..., slot_t, None, :, :],
            jnp.zeros((), chosen.dtype),
        )
        total = term if total is None else total + term
    return total


def term_maker(slab, slab_cols, local_b, local_bcols, pattern):
    total_rows = slab.shape[0]
    slots = slab.shape[2]
    width = slab.shape[3]
    slab = slab.reshape(total_rows, slots, width, width)
    slab_cols = slab_cols.reshape(total_rows, slots)

    def partial_term(start, count):
        group = math.gcd(count, 2)

        def one_group(index):
            first = index * group
            left = lax.dynamic_slice_in_dim(slab, first, group, 0)
            where_k = lax.dynamic_slice_in_dim(slab_cols, first, group, 0)
            wanted = lax.dynamic_slice_in_dim(pattern, first, group, 0)
            chosen = jnp.take(local_b, where_k, axis=0)
            chosen_cols = jnp.take(local_bcols, where_k, axis=0)
            picked = select_blocks(chosen, chosen_cols, wanted[:, None, None, :])
            return jnp.einsum("isab,iscbd->icad", left, picked, preferred_element_type=jnp.float32)

        terms = lax.map(one_group, jnp.arange(count // group, dtype=jnp.int32))
        return terms.reshape(count, pattern.shape[1], width, width)

    return partial_term


def per_device(a_blocks, a_cols, b_blocks, b_cols, c_cols):
    own_rows = a_blocks.shape[0]
    local_b = b_blocks[:, 0]
    local_bcols = b_cols[:, 0]
    pattern = c_cols[:, 0]
    per_pattern = pattern.shape[1]
    whole = lax.all_gather(a_blocks, "rep", axis=4, tiled=True)
    slab, slab_cols = (
        lax.all_to_all(whole, "blk", split_axis=1, concat_axis=0, tiled=True),
        lax.all_to_all(a_cols, "blk", split_axis=1, concat_axis=0, tiled=True),
    )
    partial_term = term_maker(slab, slab_cols, local_b, local_bcols, pattern)
    mine = lax.psum_scatter(
        partial_term(jnp.int32(0), own_rows * lax.axis_size("blk")),
        "blk",
        scatter_dimension=0,
        tiled=True,
    )
    width = a_blocks.shape[3]
    return mine.reshape(own_rows, 1, per_pattern, width, width)


def solution(mesh):
    placed = (
        P("blk", None, None, None, "rep"),
        P("blk", None, None),
        P("blk", "rep", None, None, None),
        P("blk", "rep", None),
        P(None, "rep", None),
    )
    return jax.shard_map(
        per_device,
        mesh=mesh,
        in_specs=placed,
        out_specs=P("blk", "rep", None, None, None),
        check_vma=False,
    )
```

profile of v0, /device:TPU:1, one launch (start us, length us, event | category | flops | bytes accessed | tf_op | source)
XLA Modules:
  0.0 732.5 jit_solution(5404238477490479959)
XLA Ops:
  6.5 1.9 copy.33
  8.6 17.2 %all_to_all.30 = s32[3,16,6]{2,0,1:T(4,128)S(1)} all-to-all(s32[3,16,6]{2,0,1:T(4,128)S(1)} %copy.29), channel_id=1, replica_groups=mesh['blk'=16,'rep'=16] {'blk'}, dimensions={1} | all-to-all | bytes 2304 | tf_op jit(solution)/shard_map/all_to_all | solution.py:56
  25.8 75.8 %all-gather.2.cloned.1.call-done = bf16[3,16,6,128,128]{3,4,2,0,1:T(8,128)(2,1)} async-done(((bf16[3,16,6,128,8]{3,4,2,0,1:T(8,128)(2,1)}), bf16[3,16,6,128,128]{3,4,2,0,1:T(8,128)(2,1)}) %all-gather.2.cloned.1.call-update) | async-done | bytes 9437200 | tf_op jit(solution)/shard_map/all_gather | solution.py:53
  101.6 6.9 all-to-all-start.1
  108.8 210.0 %all-to-all-done.1 = bf16[3,16,6,128,128]{3,4,2,0,1:T(8,128)(2,1)} async-done(((bf16[3,16,6,128,128]{3,4,2,0,1:T(8,128)(2,1)}), bf16[3,16,6,128,128]{3,4,2,0,1:T(8,128)(2,1)}, u32[]{:S(2)}, u32[]{:S(2)}) %all-to-all-start.1) | async-done | bytes 9437216 | tf_op jit(solution)/shard_map/all_to_all | solution.py:55
  318.8 259.3 %while.10 = (s32[]{:T(128)}, f32[24,2,4,128,128]{4,3,2,1,0:T(8,128)}, s32[24]{0:T(128)S(1)}, s32[48,6]{1,0:T(8,128)S(1)}, s32[112,3]{1,0:T(8,128)S(1)}, /*index=...) while((s32[]{:T(128)}, ...), condition=%wide.region_1.2_spmd, body=%wide.region_0.1_spmd.sunk | while | flops 205849856 | bytes 13638623 | solution.py:41
  321.0 4.9 gather_fusion.1
  331.8 4.9 gather_fusion.1
  342.6 4.9 gather_fusion.1
  353.4 4.9 gather_fusion.1
  364.2 4.9 gather_fusion.1
  375.0 4.9 gather_fusion.1
  385.9 4.9 gather_fusion.1
  396.7 4.9 gather_fusion.1
  407.5 4.9 gather_fusion.1
  418.2 4.9 gather_fusion.1
  429.0 4.9 gather_fusion.1
  439.9 4.9 gather_fusion.1
  445.8 1.6 fusion.25
  450.7 4.9 gather_fusion.1
  461.5 4.9 gather_fusion.1
  472.3 4.9 gather_fusion.1
  483.1 4.9 gather_fusion.1
  493.9 4.9 gather_fusion.1
  504.7 4.9 gather_fusion.1
  515.6 4.9 gather_fusion.1
  526.4 4.9 gather_fusion.1
  537.2 4.9 gather_fusion.1
  548.0 4.9 gather_fusion.1
  558.8 4.9 gather_fusion.1
  569.6 4.9 gather_fusion.1
  578.1 147.5 %reduce-scatter.2.cloned.1.call-done = f32[3,4,128,128]{3,2,1,0:T(8,128)} async-done(((f32[48,4,128,128]{3,2,1,0:T(8,128)}), f32[3,4,128,128]{3,2,1,0:T(8,128)}) %reduce-scatter.2.cloned.1.call-update) | async-done | bytes 786448 | tf_op jit(solution)/shard_map/reduce_scatter | solution.py:59
  (471 shorter events, 123.6 us)
Async XLA Ops:
  6.5 2.0 copy-start
  6.5 95.1 %all-gather.2.cloned.1.call-start = ((), (), s32[]{:S(2)}) async-start(), calls=%async_computation.3 | async-start | bytes 10027008 | tf_op jit(solution)/shard_map/all_gather | solution.py:53
  25.8 82.8 %copy-start.2 = (s32[112,1,3]{0,1,2:T(1,128)S(1)}, s32[112,1,3]{0,1,2:T(1,128)}, u32[]{:S(2)}) copy-start(s32[112,1,3]{0,1,2:T(1,128)} %param.10) | copy-start | bytes 4036
  25.8 82.9 %copy-start.1 = (s32[48,1,4]{0,2,1:T(4,128)S(1)}, s32[48,1,4]{0,2,1:T(4,128)}, u32[]{:S(2)}) copy-start(s32[48,1,4]{0,2,1:T(4,128)} %param.11) | copy-start | bytes 2308
  101.6 217.2 %all-to-all-start.1 = ((bf16[3,16,6,128,128]{3,4,2,0,1:T(8,128)(2,1)}), bf16[3,16,6,128,128]{3,4,2,0,1:T(8,128)(2,1)}, u32[]{:S(2)}, u32[]{:S(2)}) async-start(bf16[3,16,6,128,128]{3,4,2,0,1:T(8,128)(2,1)} %all-gather.2.cloned.1.call-done), calls=%async_computation.1 | async-start | bytes 18874368 | tf_op jit(solution)/shard_map/all_to_all | solution.py:55
  108.5 617.2 %reduce-scatter.2.cloned.1.call-start = ((), (), s32[]{:S(2)}) async-start(), calls=%async_computation.4 | async-start | bytes 13369344 | tf_op jit(solution)/shard_map/reduce_scatter | solution.py:59
Sparse Core Ops, SparseCore 0:
  10.0 91.5 all-gather.1
  578.3 147.3 reduce-scatter.1
where the time goes:
time: 735 us; the launch traced here: 733 us
  waiting for transfers between devices  433 us (59%)
  local copies, waits for them, and re-layouts  199 us (27%)
  matrix products  39 us (5%)
  blocking collectives  17.2 us (2%)
  loops' own time  16.8 us (2%)
  between operations  13.4 us (2%)
    all_to_all x1, waiting for transfers between devices, per_device(): lax.all_to_all(whole, 'blk', split_axis=1, concat_axis=0, tiled=True)  210 us
    reduce_scatter x1, waiting for transfers between devices, per_device(): lax.psum_scatter(partial_term(jnp.int32(0), own_rows * lax.axis_size('blk...  148 us
    gather x24, local copies, waits for them, and re-layouts, one_group(): chosen = jnp.take(local_b, where_k, axis=0)  118 us
    all_gather x1, waiting for transfers between devices, per_device(): whole = lax.all_gather(a_blocks, 'rep', axis=4, tiled=True)  75.8 us
    dot_general x24, matrix products, one_group(): jnp.einsum('isab,iscbd->icad', left, picked, preferred_element_type=jnp.f...  39 us
    dynamic_update_slice x48, local copies, waits for them, and re-layouts, partial_term(): terms = lax.map(one_group, jnp.arange(count // group, dtype=jnp.int32))  25.2 us
    broadcast_in_dim x120, local copies, waits for them, and re-layouts, select_blocks(): jnp.where(hits[..., slot_t, :, None, None], chosen[..., slot_t, None, :,...  18.6 us
    gather x72, local copies, waits for them, and re-layouts, one_group(): chosen_cols = jnp.take(local_bcols, where_k, axis=0)  17.6 us
  transfers between devices with their start and end apart: 3, of which 3 were waited for; matrix products, arithmetic and copies ran while one was open for 0% of the time, Pallas kernels for 0%

commit v1 on v0

--- a/solution.py
+++ b/solution.py
@@ -50,7 +50,9 @@
     local_bcols = b_cols[:, 0]
     pattern = c_cols[:, 0]
     per_pattern = pattern.shape[1]
-    whole = lax.all_gather(a_blocks, "rep", axis=4, tiled=True)
+    whole = jnp.concatenate(
+        lax.all_to_all(jnp.stack([a_blocks] * lax.axis_size("rep")), "rep", 0, 0), axis=4
+    )
     slab, slab_cols = (
         lax.all_to_all(whole, "blk", split_axis=1, concat_axis=0, tiled=True),
         lax.all_to_all(a_cols, "blk", split_axis=1, concat_axis=0, tiled=True),

time: 735 us -> 811 us (1.10)
  local copies, waits for them, and re-layouts: 199 us -> 238 us
  waiting for transfers between devices: 433 us -> 469 us
  starting transfers between devices: 6.93 us -> 24.7 us
  blocking collectives: 17.2 us -> 0 us
    all_to_all x0 -> x2, waiting for transfers between devices: none -> 107 us  [the longest x1 107 us: per_device(): lax.all_to_all(jnp.stack([a_blocks] * lax.axis_size('rep')), 'rep', 0, 0)]
    all_gather x1 -> x0, waiting for transfers between devices: 75.8 us -> none  [per_device(): whole = lax.all_gather(a_blocks, 'rep', axis=4, tiled=True)]
    all_to_all x0 -> x2, local copies, waits for them, and re-layouts: none -> 22.6 us  [the longest x1 12.7 us: per_device(): lax.all_to_all(whole, 'blk', split_axis=1, concat_axis=0, tiled=True)]
    all_to_all x1 -> x0, blocking collectives: 17.2 us -> none  [per_device(): lax.all_to_all(a_cols, 'blk', split_axis=1, concat_axis=0, tiled=True)]
    all_to_all x0 -> x2, starting transfers between devices: none -> 16.9 us  [the longest x1 8.58 us: per_device(): lax.all_to_all(jnp.stack([a_blocks] * lax.axis_size('rep')), 'rep', 0, 0)]
    reshape x0 -> x1, local copies, waits for them, and re-layouts: none -> 11.5 us  [per_device(): jnp.concatenate(lax.all_to_all(jnp.stack([a_blocks] * lax.axis_size('rep'...]
  transfers between devices with their start and end apart: 3 -> 4, of which waited for: 3 -> 3; matrix products, arithmetic and copies ran while one was open for 0% -> 3% of each run, Pallas kernels for 0% -> 0%
where the time goes in v1:
time: 811 us; the launch traced here: 808 us
  waiting for transfers between devices  469 us (58%)
  local copies, waits for them, and re-layouts  238 us (29%)
  matrix products  39 us (5%)
  starting transfers between devices  24.7 us (3%)
  loops' own time  17.3 us (2%)
  between operations  13.4 us (2%)
    all_to_all x1, waiting for transfers between devices, per_device(): lax.all_to_all(whole, 'blk', split_axis=1, concat_axis=0, tiled=True)  208 us
    reduce_scatter x1, waiting for transfers between devices, per_device(): lax.psum_scatter(partial_term(jnp.int32(0), own_rows * lax.axis_size('blk...  155 us
    gather x24, local copies, waits for them, and re-layouts, one_group(): chosen = jnp.take(local_b, where_k, axis=0)  118 us
    all_to_all x1, waiting for transfers between devices, per_device(): lax.all_to_all(jnp.stack([a_blocks] * lax.axis_size('rep')), 'rep', 0, 0)  107 us
    dot_general x24, matrix products, one_group(): jnp.einsum('isab,iscbd->icad', left, picked, preferred_element_type=jnp.f...  39 us
    dynamic_update_slice x48, local copies, waits for them, and re-layouts, partial_term(): terms = lax.map(one_group, jnp.arange(count // group, dtype=jnp.int32))  25.2 us
    broadcast_in_dim x120, local copies, waits for them, and re-layouts, select_blocks(): jnp.where(hits[..., slot_t, :, None, None], chosen[..., slot_t, None, :,...  18.6 us
    gather x72, local copies, waits for them, and re-layouts, one_group(): chosen_cols = jnp.take(local_bcols, where_k, axis=0)  17.6 us
  transfers between devices with their start and end apart: 4, of which 3 were waited for; matrix products, arithmetic and copies ran while one was open for 3% of the time, Pallas kernels for 0%

profile of v1, /device:TPU:1, one launch (start us, length us, event | category | flops | bytes accessed | tf_op | source)
XLA Modules:
  0.0 808.1 jit_solution(17557104141131425933)
XLA Ops:
  6.5 7.0 stack.2
  13.5 8.6 %all-to-all-start.1 = ((bf16[16,3,16,6,128,8]{4,5,3,2,1,0:T(8,128)(2,1)}), bf16[16,3,16,6,128,8]{4,5,3,2,1,0:T(8,128)(2,1)}, u32[]{:S(2)}, u32[]{:S(2)}) async-start(bf16[16,3,16,6,128,8]{4,5,3,2,1,0:T(8,128)(2,1)} %stack.2), calls=%async_computation.1 | async-start | bytes 18874368 | tf_op jit(solution)/shard_map/all_to_all | solution.py:54
  22.8 106.6 %all-to-all-done.1 = bf16[16,3,16,6,128,8]{4,5,3,2,1,0:T(8,128)(2,1)} async-done(((bf16[16,3,16,6,128,8]{4,5,3,2,1,0:T(8,128)(2,1)}), bf16[16,3,16,6,128,8]{4,5,3,2,1,0:T(8,128)(2,1)}, u32[]{:S(2)}, u32[]{:S(2)}) %all-to-all-start.1) | async-done | bytes 9437216 | tf_op jit(solution)/shard_map/all_to_all | solution.py:54
  129.4 8.3 %all-to-all-start = ((s32[3,16,6]{2,0,1:T(4,128)}), s32[3,16,6]{2,0,1:T(4,128)S(1)}, u32[]{:S(2)}, u32[]{:S(2)}) async-start(s32[3,16,6]{2,0,1:T(4,128)} %copy.38), calls=%async_computation | async-start | bytes 65536 | tf_op jit(solution)/shard_map/all_to_all | solution.py:58
  137.7 10.0 %copy.53 = bf16[16,3,16,6,128,8]{4,5,0,3,2,1:T(8,128)(2,1)} copy(bf16[16,3,16,6,128,8]{4,5,3,2,1,0:T(8,128)(2,1)} %all-to-all-done.1) | data formatting | bytes 18874368 | tf_op jit(solution)/shard_map/all_to_all | solution.py:54
  147.7 11.5 %copy.43 = bf16[3,16,6,128,128]{3,4,2,0,1:T(8,128)(2,1)} copy(bf16[3,16,6,128,128]{3,4,2,1,0:T(8,128)(2,1)} %bitcast.61) | data formatting | bytes 18874368 | tf_op jit(solution)/shard_map/reshape | solution.py:53
  159.2 7.7 all-to-all-start.2
  167.2 207.7 %all-to-all-done.2 = bf16[3,16,6,128,128]{3,4,2,0,1:T(8,128)(2,1)} async-done(((bf16[3,16,6,128,128]{3,4,2,0,1:T(8,128)(2,1)}), bf16[3,16,6,128,128]{3,4,2,0,1:T(8,128)(2,1)}, u32[]{:S(2)}, u32[]{:S(2)}) %all-to-all-start.2) | async-done | bytes 9437216 | tf_op jit(solution)/shard_map/all_to_all | solution.py:57
  375.0 12.7 %copy.44 = bf16[3,16,6,128,128]{4,3,2,0,1:T(8,128)(2,1)} copy(bf16[3,16,6,128,128]{3,4,2,0,1:T(8,128)(2,1)} %all-to-all-done.2) | data formatting | bytes 18874368 | tf_op jit(solution)/shard_map/all_to_all | solution.py:57
  387.6 258.9 %while.10 = (s32[]{:T(128)}, f32[24,2,4,128,128]{4,3,2,1,0:T(8,128)}, s32[24]{0:T(128)S(1)}, s32[48,6]{1,0:T(8,128)S(1)}, s32[112,3]{1,0:T(8,128)S(1)}, /*index=...) while((s32[]{:T(128)}, ...), condition=%wide.region_1.2_spmd, body=%wide.region_0.1_spmd.sunk | while | flops 205849856 | bytes 13638623 | solution.py:41
  400.6 4.9 gather_fusion.1
  411.4 4.9 gather_fusion.1
  422.2 4.9 gather_fusion.1
  433.0 4.9 gather_fusion.1
  443.8 4.9 gather_fusion.1
  454.6 4.9 gather_fusion.1
  465.4 4.9 gather_fusion.1
  476.1 4.9 gather_fusion.1
  486.9 4.9 gather_fusion.1
  497.7 4.9 gather_fusion.1
  508.5 4.9 gather_fusion.1
  519.3 4.9 gather_fusion.1
  530.1 4.9 gather_fusion.1
  540.8 4.9 gather_fusion.1
  551.6 4.9 gather_fusion.1
  562.4 4.9 gather_fusion.1
  573.2 4.9 gather_fusion.1
  584.0 4.9 gather_fusion.1
  594.8 4.9 gather_fusion.1
  605.6 4.9 gather_fusion.1
  616.4 4.9 gather_fusion.1
  646.5 154.7 %reduce-scatter.2.cloned.1.call-done = f32[3,4,128,128]{3,2,1,0:T(8,128)} async-done(((f32[48,4,128,128]{3,2,1,0:T(8,128)}), f32[3,4,128,128]{3,2,1,0:T(8,128)}) %reduce-scatter.2.cloned.1.call-update) | async-done | bytes 786448 | tf_op jit(solution)/shard_map/reduce_scatter | solution.py:61
  (474 shorter events, 139.6 us)
Async XLA Ops:
  13.5 8.6 %copy-start = (s32[3,16,6]{1,2,0:T(8,128)S(1)}, s32[3,16,6]{1,2,0:T(8,128)}, u32[]{:S(2)}) copy-start(s32[3,16,6]{1,2,0:T(8,128)} %param.8) | copy-start | bytes 3460
  13.5 115.9 %all-to-all-start.1 = ((bf16[16,3,16,6,128,8]{4,5,3,2,1,0:T(8,128)(2,1)}), bf16[16,3,16,6,128,8]{4,5,3,2,1,0:T(8,128)(2,1)}, u32[]{:S(2)}, u32[]{:S(2)}) async-start(bf16[16,3,16,6,128,8]{4,5,3,2,1,0:T(8,128)(2,1)} %stack.2), calls=%async_computation.1 | async-start | bytes 18874368 | tf_op jit(solution)/shard_map/all_to_all | solution.py:54
  129.4 29.8 %all-to-all-start = ((s32[3,16,6]{2,0,1:T(4,128)}), s32[3,16,6]{2,0,1:T(4,128)S(1)}, u32[]{:S(2)}, u32[]{:S(2)}) async-start(s32[3,16,6]{2,0,1:T(4,128)} %copy.38), calls=%async_computation | async-start | bytes 65536 | tf_op jit(solution)/shard_map/all_to_all | solution.py:58
  159.2 7.8 copy-start.2
  159.2 7.9 copy-start.1
  159.2 215.8 %all-to-all-start.2 = ((bf16[3,16,6,128,128]{3,4,2,0,1:T(8,128)(2,1)}), bf16[3,16,6,128,128]{3,4,2,0,1:T(8,128)(2,1)}, u32[]{:S(2)}, u32[]{:S(2)}) async-start(bf16[3,16,6,128,128]{3,4,2,0,1:T(8,128)(2,1)} %copy.43), calls=%async_computation.2 | async-start | bytes 18874368 | tf_op jit(solution)/shard_map/all_to_all | solution.py:57
  166.9 634.3 %reduce-scatter.2.cloned.1.call-start = ((), (), s32[]{:S(2)}) async-start(), calls=%async_computation.4 | async-start | bytes 13369344 | tf_op jit(solution)/shard_map/reduce_scatter | solution.py:61
Sparse Core Ops, SparseCore 0:
  646.7 154.5 reduce-scatter.1
